TPU v7x, 32 devices: a whole 2x2x4 slice. The times are simulated.
32 devices in a mesh: section: 2 (over x), dp: 16 (over z, y, core).
Axes of the slice: x: 2, y: 2, z: 4, core: 2. Of those that a mesh axis runs over, the one named last changes fastest.
Arguments:
- section_in: bfloat16 [2, 4, 16, 128, 1536], P('section', None, 'dp'), may hold values from -6 to 6
- top_grad: bfloat16 [4, 16, 128, 1536], P(None, 'dp'), may hold values from -0.029907227 to 0.029907227
- seq_lengths: int32 [4, 16], P(None, 'dp'), may hold values from 32 to 128, as said below
- lang_labels: int32 [4, 16], P(None, 'dp'), may hold values from 0 to 28
- norm_gain: float32 [2, 1536], P('section'), may hold values from 0.5 to 1.5
- w_down: bfloat16 [2, 1536, 256], P('section'), may hold values from -0.15625 to 0.15625
- w_up: bfloat16 [2, 256, 1536], P('section'), may hold values from -0.375 to 0.375
- critic_first: bfloat16 [1536, 768], P('section'), may hold values from -0.15625 to 0.15625
- critic_second: bfloat16 [768, 29], replicated, may hold values from -0.21875 to 0.21875
Outputs:
- grad_w_down: float32 [2, 1536, 256], P('section', 'dp')
- grad_w_up: float32 [2, 256, 1536], P('section', None, 'dp')
- grad_norm_gain: float32 [2, 1536], P('section', 'dp')
- grad_critic_first: float32 [1536, 768], P('section', 'dp')
- grad_critic_second: float32 [768, 29], P('dp')
Inputs may be any that keep to these rules, and one draw needn't show every extreme that they name: `seq_lengths`: in every draw some sequence has all 128 tokens valid.
All inputs are finite; a program needn't handle non-finite values.
Results may differ from a plain program's by a relative error of at most 0.023.
Values may be sent and summed in bfloat16 or wider, within the bound.
A program may use at most 64 MiB of HBM per device.

v0:
```python
import jax
import jax.numpy as jnp
from jax import lax
from jax.sharding import PartitionSpec as P

EPSILON = 1e-06
REVERSAL = 0.5


def from_root(array, axis, root):
    mine = lax.axis_index(axis) == root
    return lax.psum(jnp.where(mine, array, jnp.zeros_like(array)), axis)


def from_behind(block, axis, distance):
    devices = range(lax.axis_size(axis))
    route = [(i - distance, i) for i in devices if i - distance in devices]
    return lax.ppermute(block, axis, route)


def silu_slope(pre_act):
    sigma = jax.nn.sigmoid(pre_act)
    return sigma * (1.0 + pre_act * (1.0 - sigma))


def inner_rows(left, right):
    return lax.dot_general(
        left, right, (((0,), (0,)), ((), ())), preferred_element_type=jnp.float32
    )


def adapter_backward(local_rows, upstream, gain_row, down_proj, up_proj):
    values = local_rows.astype(jnp.float32)
    inv_rms = lax.rsqrt(jnp.mean(values * values, axis=-1, keepdims=True) + EPSILON)
    unit_rows = values * inv_rms
    normed = (unit_rows * gain_row[None, :]).astype(jnp.bfloat16)
    pre_act = jnp.dot(normed, down_proj, preferred_element_type=jnp.float32)
    hidden = jax.nn.silu(pre_act).astype(jnp.bfloat16)
    grad_up = inner_rows(hidden, upstream)
    grad_hidden = jnp.dot(upstream, up_proj.T, preferred_element_type=jnp.float32)
    grad_pre = (grad_hidden * silu_slope(pre_act)).astype(jnp.bfloat16)
    grad_down = inner_rows(normed, grad_pre)
    grad_normed = jnp.dot(grad_pre, down_proj.T, preferred_element_type=jnp.float32)
    grad_gain = jnp.sum(grad_normed * unit_rows, axis=0)
    scaled = grad_normed * gain_row[None, :]
    grad_input = upstream.astype(jnp.float32) + inv_rms * (
        scaled - unit_rows * jnp.mean(scaled * unit_rows, axis=-1, keepdims=True)
    )
    return (grad_input, grad_down, grad_up, grad_gain)


def critic_pass(pooled, lang_labels, critic_first, critic_second, section_place):
    batch_rows = pooled.shape[0] * pooled.shape[1]
    features = pooled.shape[2]
    values = pooled.reshape(batch_rows, features).astype(jnp.float32)
    inv_rms = lax.rsqrt(jnp.mean(values * values, axis=-1, keepdims=True) + EPSILON)
    unit_rows = values * inv_rms
    normed = unit_rows.astype(jnp.bfloat16)
    band_rows = critic_first.shape[0]
    normed_band = lax.dynamic_slice_in_dim(normed, section_place * band_rows, band_rows, 1)
    full_first = lax.all_gather(critic_first, "section", axis=0, tiled=True)
    pre_act = jnp.dot(normed, full_first, preferred_element_type=jnp.float32)
    hidden = jax.nn.silu(pre_act).astype(jnp.bfloat16)
    logits = jnp.dot(hidden, critic_second, preferred_element_type=jnp.float32)
    exponent = jnp.exp(logits)
    probabilities = exponent / jnp.sum(exponent, axis=-1, keepdims=True)
    onehot = (
        lang_labels.reshape(batch_rows)[:, None] == jnp.arange(critic_second.shape[1])[None, :]
    ).astype(jnp.float32)
    grad_logits = (probabilities - onehot).astype(jnp.bfloat16)
    grad_second = inner_rows(hidden, grad_logits)
    grad_hidden = jnp.dot(grad_logits, critic_second.T, preferred_element_type=jnp.float32)
    grad_pre = (grad_hidden * silu_slope(pre_act)).astype(jnp.bfloat16)
    grad_first = inner_rows(normed_band, grad_pre)
    grad_normed = jnp.dot(grad_pre, full_first.T, preferred_element_type=jnp.float32)
    grad_pooled = inv_rms * (
        grad_normed - unit_rows * jnp.mean(grad_normed * unit_rows, axis=-1, keepdims=True)
    )
    return (grad_first, grad_second, grad_pooled)


def body(
    section_in,
    top_grad,
    seq_lengths,
    lang_labels,
    norm_gain,
    w_down,
    w_up,
    critic_first,
    critic_second,
):
    sections = lax.axis_size("section")
    section_place = lax.axis_index("section")
    target = sections // 2
    inputs = section_in[0]
    gain_row = norm_gain[0]
    down_proj = w_down[0]
    up_proj = w_up[0]
    micro_count, seq_dev, seq_len, features = inputs.shape
    token_rows = seq_dev * seq_len
    positions = jnp.arange(seq_len)
    valid_mask = positions[None, None, :] < seq_lengths[:, :, None]
    mask_values = valid_mask.astype(jnp.float32)
    lengths = seq_lengths.astype(jnp.float32)
    totals = jnp.einsum(
        "mnt,mntd->mnd", valid_mask.astype(jnp.bfloat16), inputs, preferred_element_type=jnp.float32
    )
    pooled = (totals / lengths[:, :, None]).astype(jnp.bfloat16)
    pooled = from_root(pooled, "section", target)
    grad_first, grad_second, grad_pooled = critic_pass(
        pooled, lang_labels, critic_first, critic_second, section_place
    )
    is_target = (section_place == target).astype(jnp.float32)
    reversal = (
        -REVERSAL
        * is_target
        * grad_pooled.reshape(micro_count, seq_dev, features)
        / lengths[:, :, None]
    )
    is_last = section_place == sections - 1

    def advance(moment, carry):
        incoming, down_sum, up_sum, gain_sum = carry
        micro_now = moment - (sections - 1 - section_place)
        is_live = (micro_now >= 0) & (micro_now < micro_count)
        slot_index = jnp.clip(micro_now, 0, micro_count - 1)
        local_rows = lax.dynamic_index_in_dim(inputs, slot_index, 0, keepdims=False).reshape(
            token_rows, features
        )
        top_rows = lax.dynamic_index_in_dim(top_grad, slot_index, 0, keepdims=False).reshape(
            token_rows, features
        )
        upstream = jnp.where(is_last, top_rows, incoming)
        reverse_rows = lax.dynamic_index_in_dim(reversal, slot_index, 0, keepdims=False)
        mask_rows = lax.dynamic_index_in_dim(mask_values, slot_index, 0, keepdims=False)
        extra = (reverse_rows[:, None, :] * mask_rows[:, :, None]).reshape(token_rows, features)

        def active(operand):
            grad_input, grad_down, grad_up, grad_gain = adapter_backward(
                local_rows, upstream, gain_row, down_proj, up_proj
            )
            return ((grad_input + extra).astype(jnp.bfloat16), grad_down, grad_up, grad_gain)

        def resting(operand):
            return (
                jnp.zeros_like(incoming),
                jnp.zeros_like(down_sum),
                jnp.zeros_like(up_sum),
                jnp.zeros_like(gain_sum),
            )

        outgoing, grad_down, grad_up, grad_gain = lax.cond(is_live, active, resting, 0)
        received = from_behind(outgoing, "section", -1)
        return (received, down_sum + grad_down, up_sum + grad_up, gain_sum + grad_gain)

    initial = (
        jnp.zeros((token_rows, features), jnp.bfloat16),
        jnp.zeros(down_proj.shape, jnp.float32),
        jnp.zeros(up_proj.shape, jnp.float32),
        jnp.zeros((features,), jnp.float32),
    )
    finished = lax.fori_loop(0, micro_count + sections - 1, advance, initial)
    summed = (
        lax.psum_scatter(finished[1], "dp", scatter_dimension=0, tiled=True),
        lax.psum_scatter(finished[2], "dp", scatter_dimension=1, tiled=True),
        lax.psum_scatter(finished[3], "dp", scatter_dimension=0, tiled=True),
        lax.psum_scatter(grad_first, "dp", scatter_dimension=1, tiled=True),
        lax.psum_scatter(grad_second, "dp", scatter_dimension=0, tiled=True),
    )
    return (summed[0][None], summed[1][None], summed[2][None], summed[3], summed[4])


def solution(mesh):
    return jax.shard_map(
        body,
        mesh=mesh,
        in_specs=(
            P("section", None, "dp", None, None),
            P(None, "dp", None, None),
            P(None, "dp"),
            P(None, "dp"),
            P("section", None),
            P("section", None, None),
            P("section", None, None),
            P("section", None),
            P(),
        ),
        out_specs=(
            P("section", "dp", None),
            P("section", None, "dp"),
            P("section", "dp"),
            P("section", "dp"),
            P("dp", None),
        ),
        check_vma=False,
    )
```

profile of v0, /device:TPU:0, one launch (start us, length us, event | category | flops | bytes accessed | tf_op | source)
XLA Modules:
  0.0 345.6 jit_solution(18108459489803975215)
XLA Ops:
  7.2 0.7 all-gather.2.cloned.1.call-update
  8.0 0.7 convert_bitcast_fusion
  8.7 0.7 fusion.45
  9.4 1.7 fusion.26
  11.2 9.6 %psum.7 = bf16[4,1536]{1,0:T(4,128)(2,1)S(1)} all-reduce(bf16[4,1536]{1,0:T(4,128)(2,1)S(1)} %fusion.40), channel_id=1, replica_groups=mesh['section'=2,'dp'=16] {'section'}, use_global_device_ids=true, to_apply=%region_0.1 | all-reduce | flops 6144 | bytes 24576 | tf_op jit(solution)/shard_map/psum | solution.py:12
  21.0 27.4 %all-gather.2.cloned.1.call-done = bf16[1536,768]{1,0:T(8,128)(2,1)} async-done(((bf16[768,768]{1,0:T(8,128)(2,1)}), bf16[1536,768]{1,0:T(8,128)(2,1)}) %all-gather.2.cloned.1.call-update) | async-done | bytes 2359312 | tf_op jit(solution)/shard_map/all_gather | solution.py:61
  48.4 2.2 fusion.51
  51.1 1.0 fusion.47
  52.1 0.8 fusion.32
  53.1 0.8 broadcast.151
  54.0 93.5 %while.22 = (s32[]{:T(128)}, bf16[128,1536]{1,0:T(8,128)(2,1)}, f32[1536,256]{1,0:T(8,128)}, f32[256,1536]{1,0:T(8,128)}, f32[1536]{0:T(1024)S(1)}, /*index=5*/s...) while((s32[]{:T(128)}, bf16[128,1536]{1,0:T(8,128)(2,1)}, ...), condition=%wide.region_10.11_spmd.clone, body=%wide.region_4.10_spmd.clone.sunk | while | flops 511249024 | bytes 36070916 | solution.py:163
  54.0 1.1 conditional.3
  54.3 0.8 broadcast.138
  55.1 1.3 collective-permute-start
  56.4 1.4 select_add_fusion.6
  57.8 1.4 select_add_fusion.7
  59.2 13.3 %collective-permute-done = bf16[128,1536]{1,0:T(8,128)(2,1)} collective-permute-done((bf16[128,1536]{1,0:T(8,128)(2,1)}, bf16[128,1536]{1,0:T(8,128)(2,1)}, u32[]{:S(2)}, u32[]{:S(2)}) %collective-permute-start) | collective-permute-done | bytes 393248 | tf_op jit(solution)/shard_map/while/body/eval_jaxpr/ppermute | solution.py:18
  72.5 7.4 %conditional.3 = (bf16[128,1536]{1,0:T(8,128)(2,1)}, f32[1536,256]{1,0:T(8,128)S(1)}, f32[256,1536]{1,0:T(8,128)S(1)}, f32[1536]{0:T(1024)S(1)}) conditional(s32[]{:T(128)} %convert_element_type.158, () %tuple.70, (pred[]{:T(512)}, s32[]{:T(128)}, bf16[4,1,128,1536]{3,2,1,0:T(8,128)(2,1)}, bf16[128,1536]{1,0:T(8,128)(2,1)}, ...), branch_computations={%region_5.5_spmd, %region_6.9_spmd} | conditional | flops 509672064 | bytes 25040048 | solution.py:153
  72.5 1.2 fusion.15
  73.8 1.6 fusion.20
  75.4 1.3 bitcast_select_fusion
  78.8 1.1 fusion.13
  79.9 1.3 collective-permute-start
  81.2 2.8 select_add_fusion.6
  84.0 2.8 select_add_fusion.7
  86.8 5.8 %collective-permute-done = bf16[128,1536]{1,0:T(8,128)(2,1)} collective-permute-done((bf16[128,1536]{1,0:T(8,128)(2,1)}, bf16[128,1536]{1,0:T(8,128)(2,1)}, u32[]{:S(2)}, u32[]{:S(2)}) %collective-permute-start) | collective-permute-done | bytes 393248 | tf_op jit(solution)/shard_map/while/body/eval_jaxpr/ppermute | solution.py:18
  92.7 7.4 %conditional.3 = (bf16[128,1536]{1,0:T(8,128)(2,1)}, f32[1536,256]{1,0:T(8,128)S(1)}, f32[256,1536]{1,0:T(8,128)S(1)}, f32[1536]{0:T(1024)S(1)}) conditional(s32[]{:T(128)} %convert_element_type.158, () %tuple.70, (pred[]{:T(512)}, s32[]{:T(128)}, bf16[4,1,128,1536]{3,2,1,0:T(8,128)(2,1)}, bf16[128,1536]{1,0:T(8,128)(2,1)}, ...), branch_computations={%region_5.5_spmd, %region_6.9_spmd} | conditional | flops 509672064 | bytes 25040048 | solution.py:153
  92.7 1.2 fusion.15
  93.9 1.6 fusion.20
  95.5 1.3 bitcast_select_fusion
  98.9 1.1 fusion.13
  100.0 1.3 collective-permute-start
  101.3 2.8 select_add_fusion.6
  104.1 2.8 select_add_fusion.7
  106.9 4.9 %collective-permute-done = bf16[128,1536]{1,0:T(8,128)(2,1)} collective-permute-done((bf16[128,1536]{1,0:T(8,128)(2,1)}, bf16[128,1536]{1,0:T(8,128)(2,1)}, u32[]{:S(2)}, u32[]{:S(2)}) %collective-permute-start) | collective-permute-done | bytes 393248 | tf_op jit(solution)/shard_map/while/body/eval_jaxpr/ppermute | solution.py:18
  111.9 7.4 %conditional.3 = (bf16[128,1536]{1,0:T(8,128)(2,1)}, f32[1536,256]{1,0:T(8,128)S(1)}, f32[256,1536]{1,0:T(8,128)S(1)}, f32[1536]{0:T(1024)S(1)}) conditional(s32[]{:T(128)} %convert_element_type.158, () %tuple.70, (pred[]{:T(512)}, s32[]{:T(128)}, bf16[4,1,128,1536]{3,2,1,0:T(8,128)(2,1)}, bf16[128,1536]{1,0:T(8,128)(2,1)}, ...), branch_computations={%region_5.5_spmd, %region_6.9_spmd} | conditional | flops 509672064 | bytes 25040048 | solution.py:153
  111.9 1.2 fusion.15
  113.1 1.6 fusion.20
  114.7 1.3 bitcast_select_fusion
  118.1 1.1 fusion.13
  119.2 1.3 collective-permute-start
  120.5 2.8 select_add_fusion.6
  123.3 2.8 select_add_fusion.7
  126.1 3.9 %collective-permute-done = bf16[128,1536]{1,0:T(8,128)(2,1)} collective-permute-done((bf16[128,1536]{1,0:T(8,128)(2,1)}, bf16[128,1536]{1,0:T(8,128)(2,1)}, u32[]{:S(2)}, u32[]{:S(2)}) %collective-permute-start) | collective-permute-done | bytes 393248 | tf_op jit(solution)/shard_map/while/body/eval_jaxpr/ppermute | solution.py:18
  130.1 7.4 %conditional.3 = (bf16[128,1536]{1,0:T(8,128)(2,1)}, f32[1536,256]{1,0:T(8,128)S(1)}, f32[256,1536]{1,0:T(8,128)S(1)}, f32[1536]{0:T(1024)S(1)}) conditional(s32[]{:T(128)} %convert_element_type.158, () %tuple.70, (pred[]{:T(512)}, s32[]{:T(128)}, bf16[4,1,128,1536]{3,2,1,0:T(8,128)(2,1)}, bf16[128,1536]{1,0:T(8,128)(2,1)}, ...), branch_computations={%region_5.5_spmd, %region_6.9_spmd} | conditional | flops 509672064 | bytes 25040048 | solution.py:153
  130.1 1.2 fusion.15
  131.4 1.6 fusion.20
  133.0 1.3 bitcast_select_fusion
  136.4 1.1 fusion.13
  137.5 1.3 collective-permute-start
  138.8 2.8 select_add_fusion.6
  141.6 2.8 select_add_fusion.7
  144.4 3.1 collective-permute-done
  147.5 3.1 copy.17
  150.6 0.5 reduce-scatter.7.cloned.1.call-update
  151.2 1.9 fusion.42
  153.2 0.6 copy-done.8
  153.8 0.6 dynamic-slice
  155.0 30.1 %all-reduce = f32[1536]{0:T(1024)S(1)} all-reduce(f32[1536]{0:T(1024)S(1)} %get-tuple-element.454), channel_id=4, replica_groups=mesh['section'=2,'dp'=16] {'dp'}, use_global_device_ids=true, to_apply=%region_13.14.clone | all-reduce | flops 1536 | bytes 12288
  185.2 0.6 dynamic-slice_bitcast_fusion
  185.7 1.4 copy.21
  187.2 22.6 %reduce-scatter.9.cloned.1.call-done = f32[256,96]{0,1:T(8,128)} async-done(((f32[256,1536]{0,1:T(8,128)}), f32[256,96]{0,1:T(8,128)}) %reduce-scatter.9.cloned.1.call-update) | async-done | bytes 98320 | tf_op jit(solution)/shard_map/reduce_scatter | solution.py:166
  209.8 62.6 %reduce-scatter.7.cloned.1.call-done = f32[96,256]{1,0:T(8,128)} async-done(((f32[1536,256]{1,0:T(8,128)}), f32[96,256]{1,0:T(8,128)}) %reduce-scatter.7.cloned.1.call-update) | async-done | bytes 98320 | tf_op jit(solution)/shard_map/reduce_scatter | solution.py:165
  272.4 66.7 %reduce-scatter.11.cloned.1.call-done = f32[768,48]{0,1:T(8,128)} async-done(((f32[768,768]{0,1:T(8,128)}), f32[768,48]{0,1:T(8,128)}) %reduce-scatter.11.cloned.1.call-update) | async-done | bytes 147472 | tf_op jit(solution)/shard_map/reduce_scatter | solution.py:168
  (105 shorter events, 10.2 us)
Async XLA Ops:
  7.2 43.4 %copy-start = (bf16[768,29]{0,1:T(8,128)(2,1)S(1)}, bf16[768,29]{0,1:T(8,128)(2,1)}, u32[]{:S(2)}) copy-start(bf16[768,29]{0,1:T(8,128)(2,1)} %param.21) | copy-start | bytes 133636
  7.2 41.2 %all-gather.2.cloned.1.call-start = ((), (), s32[]{:S(2)}) async-start(), calls=%async_computation.4 | async-start | bytes 3538944 | tf_op jit(solution)/shard_map/all_gather | solution.py:61
  7.9 177.8 %reduce-scatter.13.cloned.1.call-start = ((), (), s32[]{:S(2)}) async-start(), calls=%async_computation.8 | async-start | bytes 417792
  11.1 39.8 %copy-start.6 = (s32[4,1]{0,1:T(1,128)S(1)}, s32[4,1]{0,1:T(1,128)}, u32[]{:S(2)}) copy-start(s32[4,1]{0,1:T(1,128)} %param.16) | copy-start | bytes 52
  48.4 3.7 %copy-start.3 = (bf16[1536,768]{1,0:T(8,128)(2,1)S(1)}, bf16[1536,768]{1,0:T(8,128)(2,1)}, u32[]{:S(2)}) copy-start(bf16[1536,768]{1,0:T(8,128)(2,1)} %all-gather.2.cloned.1.call-done) | copy-start | bytes 7077892
  52.1 1.9 copy-start.4
  52.1 1.9 copy-start.5
  53.1 156.7 %reduce-scatter.9.cloned.1.call-start = ((), (), s32[]{:S(2)}) async-start(), calls=%async_computation.6 | async-start | bytes 1671168 | tf_op jit(solution)/shard_map/reduce_scatter | solution.py:166
  55.1 17.4 %collective-permute-start = (bf16[128,1536]{1,0:T(8,128)(2,1)}, bf16[128,1536]{1,0:T(8,128)(2,1)}, u32[]{:S(2)}, u32[]{:S(2)}) collective-permute-start(bf16[128,1536]{1,0:T(8,128)(2,1)} %get-tuple-element.659), channel_id=1, source_target_pairs={{16,0},{17,1},{18,2},{19,3},{20,4},{21,5},{22,6},{23,7},{24,8},{25... | collective-permute-start | bytes 1179656 | tf_op jit(solution)/shard_map/while/body/eval_jaxpr/ppermute | solution.py:18
  72.5 4.2 %copy-start.7 = (bf16[256,1536]{1,0:T(8,128)(2,1)S(1)}, bf16[256,1536]{1,0:T(8,128)(2,1)}, u32[]{:S(2)}) copy-start(bf16[256,1536]{1,0:T(8,128)(2,1)} %get-tuple-element.420) | copy-start | bytes 2359300 | tf_op jit(solution)/shard_map/while/body/eval_jaxpr/cond
  75.4 1.7 copy-start.1
  77.1 1.1 copy-start.2
  79.9 12.7 %collective-permute-start = (bf16[128,1536]{1,0:T(8,128)(2,1)}, bf16[128,1536]{1,0:T(8,128)(2,1)}, u32[]{:S(2)}, u32[]{:S(2)}) collective-permute-start(bf16[128,1536]{1,0:T(8,128)(2,1)} %get-tuple-element.659), channel_id=1, source_target_pairs={{16,0},{17,1},{18,2},{19,3},{20,4},{21,5},{22,6},{23,7},{24,8},{25... | collective-permute-start | bytes 1179656 | tf_op jit(solution)/shard_map/while/body/eval_jaxpr/ppermute | solution.py:18
  92.7 4.2 %copy-start.7 = (bf16[256,1536]{1,0:T(8,128)(2,1)S(1)}, bf16[256,1536]{1,0:T(8,128)(2,1)}, u32[]{:S(2)}) copy-start(bf16[256,1536]{1,0:T(8,128)(2,1)} %get-tuple-element.420) | copy-start | bytes 2359300 | tf_op jit(solution)/shard_map/while/body/eval_jaxpr/cond
  95.5 1.7 copy-start.1
  97.2 1.1 copy-start.2
  100.0 11.7 %collective-permute-start = (bf16[128,1536]{1,0:T(8,128)(2,1)}, bf16[128,1536]{1,0:T(8,128)(2,1)}, u32[]{:S(2)}, u32[]{:S(2)}) collective-permute-start(bf16[128,1536]{1,0:T(8,128)(2,1)} %get-tuple-element.659), channel_id=1, source_target_pairs={{16,0},{17,1},{18,2},{19,3},{20,4},{21,5},{22,6},{23,7},{24,8},{25... | collective-permute-start | bytes 1179656 | tf_op jit(solution)/shard_map/while/body/eval_jaxpr/ppermute | solution.py:18
  111.9 4.2 %copy-start.7 = (bf16[256,1536]{1,0:T(8,128)(2,1)S(1)}, bf16[256,1536]{1,0:T(8,128)(2,1)}, u32[]{:S(2)}) copy-start(bf16[256,1536]{1,0:T(8,128)(2,1)} %get-tuple-element.420) | copy-start | bytes 2359300 | tf_op jit(solution)/shard_map/while/body/eval_jaxpr/cond
  114.7 1.7 copy-start.1
  116.4 1.1 copy-start.2
  119.2 10.8 %collective-permute-start = (bf16[128,1536]{1,0:T(8,128)(2,1)}, bf16[128,1536]{1,0:T(8,128)(2,1)}, u32[]{:S(2)}, u32[]{:S(2)}) collective-permute-start(bf16[128,1536]{1,0:T(8,128)(2,1)} %get-tuple-element.659), channel_id=1, source_target_pairs={{16,0},{17,1},{18,2},{19,3},{20,4},{21,5},{22,6},{23,7},{24,8},{25... | collective-permute-start | bytes 1179656 | tf_op jit(solution)/shard_map/while/body/eval_jaxpr/ppermute | solution.py:18
  130.1 4.2 %copy-start.7 = (bf16[256,1536]{1,0:T(8,128)(2,1)S(1)}, bf16[256,1536]{1,0:T(8,128)(2,1)}, u32[]{:S(2)}) copy-start(bf16[256,1536]{1,0:T(8,128)(2,1)} %get-tuple-element.420) | copy-start | bytes 2359300 | tf_op jit(solution)/shard_map/while/body/eval_jaxpr/cond
  133.0 1.7 copy-start.1
  134.7 1.1 copy-start.2
  137.5 10.0 %collective-permute-start = (bf16[128,1536]{1,0:T(8,128)(2,1)}, bf16[128,1536]{1,0:T(8,128)(2,1)}, u32[]{:S(2)}, u32[]{:S(2)}) collective-permute-start(bf16[128,1536]{1,0:T(8,128)(2,1)} %get-tuple-element.659), channel_id=1, source_target_pairs={{16,0},{17,1},{18,2},{19,3},{20,4},{21,5},{22,6},{23,7},{24,8},{25... | collective-permute-start | bytes 1179656 | tf_op jit(solution)/shard_map/while/body/eval_jaxpr/ppermute | solution.py:18
  150.6 121.8 %reduce-scatter.7.cloned.1.call-start = ((), (), s32[]{:S(2)}) async-start(), calls=%async_computation.5 | async-start | bytes 1671168 | tf_op jit(solution)/shard_map/reduce_scatter | solution.py:165
  151.1 187.9 %reduce-scatter.11.cloned.1.call-start = ((), (), s32[]{:S(2)}) async-start(), calls=%async_computation.7 | async-start | bytes 2506752 | tf_op jit(solution)/shard_map/reduce_scatter | solution.py:168
  153.1 0.7 copy-start.8
Sparse Core Ops, SparseCore 0:
  9.6 38.7 all-gather.1
  53.2 55.6 reduce-scatter.12
  150.7 59.0 reduce-scatter.8
  213.8 58.4 reduce-scatter.6
  277.0 61.9 reduce-scatter.10
where the time goes:
time: 347 us; the launch traced here: 346 us
  waiting for transfers between devices  211 us (61%)
  other arithmetic  41.9 us (12%)
  blocking collectives  39.7 us (11%)
  matrix products  21.5 us (6%)
  between operations  14.5 us (4%)
  local copies, waits for them, and re-layouts  9.4 us (3%)
  starting transfers between devices  6.6 us (2%)
    reduce_scatter x1, waiting for transfers between devices, body(): lax.psum_scatter(grad_first, 'dp', scatter_dimension=1, tiled=True)  66.7 us
    reduce_scatter x1, waiting for transfers between devices, body(): lax.psum_scatter(finished[1], 'dp', scatter_dimension=0, tiled=True)  62.6 us
    ppermute x5, waiting for transfers between devices, from_behind(): return lax.ppermute(block, axis, route)  31 us
    unnamed x1, blocking collectives  30.1 us
    all_gather x1, waiting for transfers between devices, critic_pass(): full_first = lax.all_gather(critic_first, 'section', axis=0, tiled=True)  27.4 us
    reduce_scatter x1, waiting for transfers between devices, body(): lax.psum_scatter(finished[2], 'dp', scatter_dimension=1, tiled=True)  22.6 us
    add x5, other arithmetic, advance(): up_sum + grad_up  12.6 us
    add x5, other arithmetic, advance(): down_sum + grad_down  12.5 us
  transfers between devices with their start and end apart: 10, of which 9 were waited for; matrix products, arithmetic and copies ran while one was open for 19% of the time, Pallas kernels for 0%

commit v1 on v0

--- a/solution.py
+++ b/solution.py
@@ -1,10 +1,473 @@
+import functools
+
 import jax
 import jax.numpy as jnp
 from jax import lax
+from jax.experimental import pallas as pl
+from jax.experimental.pallas import tpu as pltpu
 from jax.sharding import PartitionSpec as P
 
 EPSILON = 1e-06
 REVERSAL = 0.5
+PAD = 16
+LANES = 128
+F32 = jnp.float32
+BF16 = jnp.bfloat16
+MESH = pl.DeviceIdType.MESH
+
+
+def contract(left, right, left_dim, right_dim):
+    return lax.dot_general(
+        left, right, (((left_dim,), (right_dim,)), ((), ())), preferred_element_type=F32
+    )
+
+
+def bit_orders(bits):
+    near = list(range(bits))
+    return near, ([0] + near[2:] + [1] if bits > 1 else near)
+
+
+def relay_kernel(
+    sizes,
+    lengths_ref,
+    labels_ref,
+    x_ref,
+    g_ref,
+    gain_ref,
+    gain_cut_ref,
+    wd_ref,
+    wu_ref,
+    cf_ref,
+    cs_ref,
+    gwd_ref,
+    gwu_ref,
+    gain_out_ref,
+    first_ref,
+    second_ref,
+    *scratch,
+):
+    micro, length, bits, chunk = sizes
+    (
+        xn_ref,
+        g0_ref,
+        h_ref,
+        da_ref,
+        slope_ref,
+        wu_in_ref,
+        h0_ref,
+        p_ref,
+        p_in_ref,
+        pool_ref,
+        pre_ref,
+        pre_in_ref,
+        gn_ref,
+        gn_in_ref,
+        cs_pad_ref,
+        pack32_ref,
+        ag_ref,
+        last_ref,
+        last_in_ref,
+        *job_refs,
+        x_sems,
+        ag_sems,
+        rs_sems,
+    ) = scratch
+    dp = 1 << bits
+    tokens, features = x_ref.shape
+    rank = wd_ref.shape[1]
+    band, hidden_width = cf_ref.shape
+    languages = cs_ref.shape[1]
+    cut = features // dp
+    section = lax.axis_index("section")
+    replica = lax.axis_index("dp")
+    across = (1 - section, replica)
+
+    def peer(bit):
+        mine = lax.rem(replica // (1 << bit), 2)
+        return mine, (section, replica + (1 - 2 * mine) * (1 << bit))
+
+    orders = bit_orders(bits)
+    job_order = (orders[0], orders[1], orders[0])
+    cuts = [job_refs[job * 2 * bits : job * 2 * bits + bits] for job in range(3)]
+    lands = [job_refs[job * 2 * bits + bits : (job + 1) * 2 * bits] for job in range(3)]
+
+    def x_copy(slot, src, dst, device):
+        return pltpu.make_async_remote_copy(
+            src_ref=src,
+            dst_ref=dst,
+            send_sem=x_sems.at[2 * slot],
+            recv_sem=x_sems.at[2 * slot + 1],
+            device_id=device,
+            device_id_type=MESH,
+        )
+
+    core, beside = peer(0)
+    half_rank = rank // 2
+    my_half = wu_ref.at[pl.ds(pl.multiple_of(core * half_rank, half_rank), half_rank)]
+    my_half_in = wu_in_ref.at[pl.ds(pl.multiple_of(core * half_rank, half_rank), half_rank)]
+    up_across = x_copy(0, my_half, my_half_in, across)
+    up_beside = x_copy(1, my_half_in, my_half_in, beside)
+    pool_across = x_copy(2, pool_ref, pool_ref, across)
+    pre_across = x_copy(3, pre_ref, pre_in_ref, across)
+    gn_across = x_copy(4, gn_ref, gn_in_ref, across)
+    h_across = x_copy(5, h_ref, h0_ref, across)
+    p_across = x_copy(6, p_ref, p_in_ref, across)
+    last_across = x_copy(7, last_ref, last_in_ref, across)
+
+    def ag_copy(step):
+        count = 1 << step
+        return pltpu.make_async_remote_copy(
+            src_ref=ag_ref.at[pl.ds(0, count)],
+            dst_ref=ag_ref.at[pl.ds(count, count)],
+            send_sem=ag_sems.at[2 * step],
+            recv_sem=ag_sems.at[2 * step + 1],
+            device_id=peer(bits - 1 - step)[1],
+            device_id_type=MESH,
+        )
+
+    def rs_copy(job, step):
+        count = dp >> (step + 1)
+        mine, other = peer(job_order[job][step])
+        return pltpu.make_async_remote_copy(
+            src_ref=cuts[job][step].at[pl.ds((1 - mine) * count, count)],
+            dst_ref=lands[job][step],
+            send_sem=rs_sems.at[2 * (job * bits + step)],
+            recv_sem=rs_sems.at[2 * (job * bits + step) + 1],
+            device_id=other,
+            device_id_type=MESH,
+        )
+
+    def rs_take(job, step):
+        count = dp >> (step + 1)
+        mine = peer(job_order[job][step])[0]
+        rs_copy(job, step).wait_recv()
+        kept = cuts[job][step][pl.ds(mine * count, count)].astype(F32)
+        return kept + lands[job][step][...].astype(F32)
+
+    def rs_step(job, step):
+        cuts[job][step + 1][...] = rs_take(job, step).astype(BF16)
+        rs_copy(job, step + 1).start()
+
+    def fill(job, left_ref, right_ref, extra=None):
+        group = 4 * cut
+        for part in range(features // group):
+            columns = pl.ds(part * group, group)
+            product = contract(left_ref[:, columns], right_ref[...], 0, 0)
+            if extra is not None:
+                product += contract(
+                    extra[0][:, part * group : (part + 1) * group], extra[1], 0, 0
+                )
+            product = product.astype(BF16)
+            for inner in range(4):
+                target = part * 4 + inner
+                place = 0
+                for step, bit in enumerate(job_order[job]):
+                    place += ((target >> bit) & 1) << (bits - 1 - step)
+                cuts[job][0][place] = product[inner * cut : (inner + 1) * cut]
+
+    barrier = pltpu.get_barrier_semaphore()
+    pl.semaphore_signal(barrier, inc=1, device_id=across, device_id_type=MESH)
+    for bit in range(bits):
+        pl.semaphore_signal(barrier, inc=1, device_id=peer(bit)[1], device_id_type=MESH)
+    pl.semaphore_wait(barrier, bits + 1)
+
+    row_of = lax.broadcasted_iota(jnp.int32, (PAD, tokens), 0)
+    token_of = lax.broadcasted_iota(jnp.int32, (PAD, tokens), 1)
+    valid = jnp.zeros((PAD, tokens), F32)
+    pad_rows = lax.broadcasted_iota(jnp.int32, (PAD, 1), 0)
+    lengths = jnp.ones((PAD, 1), F32)
+    labels = jnp.full((PAD, 1), -1, jnp.int32)
+    for m in range(micro):
+        seq = lengths_ref[m, 0]
+        inside = (row_of == m) & (token_of >= m * length) & (token_of < m * length + seq)
+        valid = jnp.where(inside, 1.0, valid)
+        lengths = jnp.where(pad_rows == m, seq.astype(F32), lengths)
+        labels = jnp.where(pad_rows == m, labels_ref[m, 0], labels)
+    valid = valid.astype(BF16)
+
+    def normalised(rows):
+        values = x_ref[rows, :].astype(F32)
+        inv_rms = lax.rsqrt(jnp.mean(values * values, axis=-1, keepdims=True) + EPSILON)
+        unit = values * inv_rms
+        xn = (unit * gain_ref[...]).astype(BF16)
+        xn_ref[rows, :] = xn
+        pre_act = contract(xn, wd_ref[...], 1, 0)
+        sigma = jax.nn.sigmoid(pre_act)
+        h_ref[rows, :] = (pre_act * sigma).astype(BF16)
+        return inv_rms, unit, sigma * (1.0 + pre_act * (1.0 - sigma))
+
+    @pl.when(section == 0)
+    def _():
+        up_across.start()
+
+        @pl.loop(0, tokens // chunk)
+        def _(index):
+            rows = pl.ds(pl.multiple_of(index * chunk, chunk), chunk)
+            slope_ref[rows, :] = normalised(rows)[2]
+
+        h_across.start()
+        pool_across.wait_recv()
+
+    @pl.when(section == 1)
+    def _():
+        totals = contract(valid, x_ref[...], 1, 0)
+        pool_ref[...] = (totals / lengths).astype(BF16)
+        pool_across.start()
+
+    pooled = pool_ref[...].astype(F32)
+    pooled_inv = lax.rsqrt(jnp.mean(pooled * pooled, axis=-1, keepdims=True) + EPSILON)
+    pooled_unit = pooled * pooled_inv
+    pooled_normed = jnp.where(section == 0, pooled_unit[:, :band], pooled_unit[:, band:])
+    pre_ref[...] = contract(pooled_normed.astype(BF16), cf_ref[...], 1, 0)
+    pre_across.start()
+    cs_pad_ref[...] = jnp.zeros(cs_pad_ref.shape, BF16)
+    cs_pad_ref[:, :languages] = cs_ref[...]
+
+    @pl.when(section == 1)
+    def _():
+        @pl.loop(0, tokens // chunk)
+        def _(index):
+            rows = pl.ds(pl.multiple_of(index * chunk, chunk), chunk)
+            inv_rms, unit, slope = normalised(rows)
+            upstream = g_ref[rows, :]
+            grad_hidden = contract(upstream, wu_ref[...], 1, 1)
+            da = (grad_hidden * slope).astype(BF16)
+            da_ref[rows, :] = da
+            scaled = contract(da, wd_ref[...], 1, 1) * gain_ref[...]
+            tilt = jnp.mean(scaled * unit, axis=-1, keepdims=True)
+            g0_ref[rows, :] = (
+                upstream.astype(F32) + inv_rms * (scaled - unit * tilt)
+            ).astype(BF16)
+
+        fill(0, xn_ref, da_ref)
+        rs_copy(0, 0).start()
+        fill(1, g_ref, h_ref)
+        rs_copy(1, 0).start()
+        up_across.wait_recv()
+        up_beside.start()
+
+    pre_across.wait_recv()
+    pre = pre_ref[...] + pre_in_ref[...]
+    sigma = jax.nn.sigmoid(pre)
+    hidden = (pre * sigma).astype(BF16)
+    logits = contract(hidden, cs_pad_ref[...], 1, 0)
+    language = lax.broadcasted_iota(jnp.int32, (PAD, LANES), 1)
+    exponent = jnp.where(language < languages, jnp.exp(logits), 0.0)
+    probabilities = exponent / jnp.sum(exponent, axis=-1, keepdims=True)
+    onehot = jnp.where(language == labels, 1.0, 0.0)
+    grad_logits = (probabilities - onehot).astype(BF16)
+    grad_hidden = contract(grad_logits, cs_pad_ref[...], 1, 1)
+    grad_pre = (grad_hidden * (sigma * (1.0 + pre * (1.0 - sigma)))).astype(BF16)
+    gn_ref[...] = contract(grad_pre, cf_ref[...], 1, 1)
+
+    @pl.when(section == 0)
+    def _():
+        gn_across.start()
+
+    pack32_ref[...] = jnp.zeros(pack32_ref.shape, F32)
+    pack32_ref[0:micro, :band] = pooled_normed[:micro]
+    pack32_ref[micro : 2 * micro, :hidden_width] = hidden.astype(F32)[:micro]
+    pack32_ref[2 * micro : 3 * micro, :hidden_width] = grad_pre.astype(F32)[:micro]
+    pack32_ref[3 * micro : 4 * micro, :LANES] = grad_logits.astype(F32)[:micro]
+    ag_ref[0] = pack32_ref[...].astype(BF16)
+    ag_copy(0).start()
+
+    @pl.when(section == 1)
+    def _():
+        gn_across.wait_recv()
+        grad_normed = jnp.concatenate([gn_in_ref[...], gn_ref[...]], axis=1)
+        tilt = jnp.mean(grad_normed * pooled_unit, axis=-1, keepdims=True)
+        grad_pooled = pooled_inv * (grad_normed - pooled_unit * tilt)
+        in_use = pad_rows < micro
+        reversal = jnp.where(in_use, -REVERSAL * grad_pooled / lengths, 0.0).astype(BF16)
+        up_beside.wait_recv()
+        up_reversal = contract(reversal, wu_in_ref[...], 1, 1)
+        for m in range(micro):
+            rows = pl.ds(m * length, length)
+            inside = lax.broadcasted_iota(jnp.int32, (length, 1), 0) < lengths_ref[m, 0]
+            extra = jnp.where(inside, up_reversal[m : m + 1], 0.0)
+            p_ref[rows, :] = (contract(g0_ref[rows, :], wu_in_ref[...], 1, 1) + extra).astype(BF16)
+        p_across.start()
+        rs_step(0, 0)
+        rs_step(1, 0)
+        h_across.wait_recv()
+        masked_h = contract(valid, h0_ref[...], 1, 0).astype(BF16)
+        fill(2, g0_ref, h0_ref, (reversal, masked_h))
+        rs_copy(2, 0).start()
+
+    def ag_step(step):
+        ag_copy(step).wait_recv()
+        if step + 1 < bits:
+            ag_copy(step + 1).start()
+
+    def critic_outputs():
+        blocks = ag_ref[...].reshape(dp * PAD, ag_ref.shape[2])
+        total = dp * PAD
+        from_row = lax.broadcasted_iota(jnp.int32, (total, total), 1)
+        to_row = lax.broadcasted_iota(jnp.int32, (total, total), 0)
+        early = lax.rem(to_row, PAD) < 2 * micro
+        shift = jnp.where(early & (from_row == to_row + 2 * micro), 1.0, 0.0).astype(BF16)
+        own = hidden_width // dp
+        at = lax.broadcasted_iota(jnp.int32, (blocks.shape[1], LANES), 0)
+        lane = lax.broadcasted_iota(jnp.int32, (blocks.shape[1], LANES), 1)
+        pick = jnp.where((at == lane + replica * own) & (lane < own), 1.0, 0.0).astype(BF16)
+        picked = contract(blocks, pick, 1, 0)
+        place = lax.rem(lax.broadcasted_iota(jnp.int32, (total, LANES), 0), PAD)
+        moved_pre = contract(shift, picked.astype(BF16), 1, 0)
+        moved_pre = jnp.where(place < micro, moved_pre, 0.0).astype(BF16)
+        moved_logits = contract(shift, blocks[:, :LANES], 1, 0).astype(BF16)
+        hidden_own = jnp.where((place >= micro) & (place < 2 * micro), picked, 0.0).astype(BF16)
+        first_ref[...] = contract(blocks[:, :band], moved_pre, 0, 0)[:, :own]
+        second_ref[...] = contract(hidden_own, moved_logits, 0, 0)[:own, :languages]
+
+    def finish_down():
+        reduced = rs_take(0, bits - 1)[0]
+        gwd_ref[...] = reduced
+        start = pl.multiple_of(replica * cut, cut)
+        weighted = reduced * wd_ref[pl.ds(start, cut), :].astype(F32)
+        row = lax.dot_general(
+            jnp.ones((8, rank), F32),
+            weighted,
+            (((1,), (1,)), ((), ())),
+            precision=lax.Precision.HIGHEST,
+            preferred_element_type=F32,
+        )
+        gain_out_ref[...] = row[0:1] / gain_cut_ref[pl.ds(replica, 1), :]
+
+    @pl.when(section == 1)
+    def _():
+        for step in range(bits):
+            ag_step(step)
+            if step + 1 < bits:
+                rs_step(2, step)
+            if step + 2 < bits:
+                rs_step(0, step + 1)
+                rs_step(1, step + 1)
+        last_ref[...] = rs_take(2, bits - 1)[0]
+        last_across.start()
+        finish_down()
+        gwu_ref[...] = rs_take(1, bits - 1)[0]
+        critic_outputs()
+
+    @pl.when(section == 0)
+    def _():
+        for step in range(bits):
+            ag_step(step)
+        critic_outputs()
+        p_across.wait_recv()
+        da_ref[...] = (p_in_ref[...].astype(F32) * slope_ref[...]).astype(BF16)
+        fill(0, xn_ref, da_ref)
+        rs_copy(0, 0).start()
+        for step in range(bits - 1):
+            rs_step(0, step)
+        finish_down()
+        last_across.wait_recv()
+        gwu_ref[...] = last_in_ref[...]
+
+    pre_across.wait_send()
+    for step in range(bits):
+        ag_copy(step).wait_send()
+        rs_copy(0, step).wait_send()
+
+    @pl.when(section == 0)
+    def _():
+        up_across.wait_send()
+        h_across.wait_send()
+        gn_across.wait_send()
+
+    @pl.when(section == 1)
+    def _():
+        up_beside.wait_send()
+        pool_across.wait_send()
+        p_across.wait_send()
+        last_across.wait_send()
+        for step in range(bits):
+            rs_copy(1, step).wait_send()
+            rs_copy(2, step).wait_send()
+
+
+def fused_body(
+    section_in,
+    top_grad,
+    seq_lengths,
+    lang_labels,
+    norm_gain,
+    w_down,
+    w_up,
+    critic_first,
+    critic_second,
+):
+    dp = lax.axis_size("dp")
+    bits = dp.bit_length() - 1
+    micro, _, length, features = section_in.shape[1:]
+    tokens = micro * length
+    rank = w_down.shape[2]
+    band, hidden_width = critic_first.shape
+    languages = critic_second.shape[1]
+    cut = features // dp
+    width = max(band, hidden_width)
+    chunk = min(2 * length, tokens)
+    jobs = []
+    for _ in range(3):
+        jobs += [pltpu.VMEM((dp >> step, cut, rank), BF16) for step in range(bits)]
+        jobs += [pltpu.VMEM((dp >> (step + 1), cut, rank), BF16) for step in range(bits)]
+    vmem = pl.BlockSpec(memory_space=pltpu.VMEM)
+    smem = pl.BlockSpec(memory_space=pltpu.SMEM)
+    gwd, gwu, gain, first, second = pl.pallas_call(
+        functools.partial(relay_kernel, (micro, length, bits, chunk)),
+        out_shape=(
+            jax.ShapeDtypeStruct((cut, rank), F32),
+            jax.ShapeDtypeStruct((cut, rank), F32),
+            jax.ShapeDtypeStruct((1, cut), F32),
+            jax.ShapeDtypeStruct((band, hidden_width // dp), F32),
+            jax.ShapeDtypeStruct((hidden_width // dp, languages), F32),
+        ),
+        in_specs=[smem, smem] + [vmem] * 8,
+        out_specs=(vmem,) * 5,
+        scratch_shapes=[
+            pltpu.VMEM((tokens, features), BF16),
+            pltpu.VMEM((tokens, features), BF16),
+            pltpu.VMEM((tokens, rank), BF16),
+            pltpu.VMEM((tokens, rank), BF16),
+            pltpu.VMEM((tokens, rank), F32),
+            pltpu.VMEM((rank, features), BF16),
+            pltpu.VMEM((tokens, rank), BF16),
+            pltpu.VMEM((tokens, rank), BF16),
+            pltpu.VMEM((tokens, rank), BF16),
+            pltpu.VMEM((PAD, features), BF16),
+            pltpu.VMEM((PAD, hidden_width), F32),
+            pltpu.VMEM((PAD, hidden_width), F32),
+            pltpu.VMEM((PAD, band), F32),
+            pltpu.VMEM((PAD, band), F32),
+            pltpu.VMEM((hidden_width, LANES), BF16),
+            pltpu.VMEM((PAD, width), F32),
+            pltpu.VMEM((dp, PAD, width), BF16),
+            pltpu.VMEM((cut, rank), F32),
+            pltpu.VMEM((cut, rank), F32),
+            *jobs,
+            pltpu.SemaphoreType.DMA((16,)),
+            pltpu.SemaphoreType.DMA((2 * bits,)),
+            pltpu.SemaphoreType.DMA((6 * bits,)),
+        ],
+        compiler_params=pltpu.CompilerParams(
+            collective_id=0, has_side_effects=True, vmem_limit_bytes=52 * 2**20
+        ),
+        cost_estimate=pl.CostEstimate(
+            flops=12 * tokens * features * rank, bytes_accessed=8 * 2**20, transcendentals=0
+        ),
+    )(
+        seq_lengths,
+        lang_labels,
+        section_in.reshape(tokens, features),
+        top_grad.reshape(tokens, features),
+        norm_gain,
+        norm_gain.reshape(dp, cut),
+        w_down[0],
+        w_up[0],
+        critic_first,
+        critic_second,
+    )
+    return (gwd[None], gwu.T[None], gain, first, second)
 
 
 def from_root(array, axis, root):
@@ -172,8 +635,26 @@
 
 
 def solution(mesh):
+    sections, replicas = mesh.shape["section"], mesh.shape["dp"]
+
+    def program(*args):
+        micro, sequences = args[2].shape
+        fits = (
+            sections == 2
+            and sequences == replicas
+            and replicas >= 4
+            and replicas & (replicas - 1) == 0
+            and micro * 4 == PAD
+            and args[4].shape[1] % (replicas * PAD) == 0
+        )
+        return placed(mesh, fused_body if fits else body)(*args)
+
+    return program
+
+
+def placed(mesh, device_body):
     return jax.shard_map(
-        body,
+        device_body,
         mesh=mesh,
         in_specs=(
             P("section", None, "dp", None, None),

time: 347 us -> 58.8 us (0.17)
  waiting for transfers between devices: 211 us -> 0 us
  Pallas kernels: 0 us -> 49.5 us
  other arithmetic: 41.9 us -> 0.71 us
  blocking collectives: 39.7 us -> 0 us
  matrix products: 21.5 us -> 0 us
  between operations: 14.5 us -> 0.66 us
  starting transfers between devices: 6.6 us -> 0 us
    reduce_scatter x3 -> x0, waiting for transfers between devices: 152 us -> none  [the longest x1 66.7 us: body(): lax.psum_scatter(grad_first, 'dp', scatter_dimension=1, tiled=True)]
    pallas_call x0 -> x1, Pallas kernels: none -> 49.5 us  [fused_body(): pl.pallas_call(functools.partial(relay_kernel, (micro, length, bits, chun...]
    ppermute x5 -> x0, waiting for transfers between devices: 31 us -> none  [from_behind(): return lax.ppermute(block, axis, route)]
    unnamed x1 -> x0, blocking collectives: 30.1 us -> none
    all_gather x1 -> x0, waiting for transfers between devices: 27.4 us -> none  [critic_pass(): full_first = lax.all_gather(critic_first, 'section', axis=0, tiled=True)]
    add x15 -> x0, other arithmetic: 25.1 us -> none  [the longest x5 12.6 us: advance(): up_sum + grad_up]
    dot_general x26 -> x0, matrix products: 20.5 us -> none  [the longest x4 6.31 us: adapter_backward(): pre_act = jnp.dot(normed, down_proj, preferred_element_type=jnp.float32)]
    psum x1 -> x0, blocking collectives: 9.59 us -> none  [from_root(): return lax.psum(jnp.where(mine, array, jnp.zeros_like(array)), axis)]
  transfers between devices with their start and end apart: 10 -> 0, of which waited for: 9 -> 0; matrix products, arithmetic and copies ran while one was open for 19% -> 0% of each run, Pallas kernels for 0% -> 0%
where the time goes in v1:
time: 58.8 us; the launch traced here: 58.5 us
  Pallas kernels  49.5 us (84%)
  local copies, waits for them, and re-layouts  7.63 us (13%)
  other arithmetic  0.71 us (1%)
  between operations  0.66 us (1%)
    pallas_call x1, Pallas kernels, fused_body(): pl.pallas_call(functools.partial(relay_kernel, (micro, length, bits, chun...  49.5 us
    unnamed x12, local copies, waits for them, and re-layouts  7.56 us

profile of v1, /device:TPU:0, one launch (start us, length us, event | category | flops | bytes accessed | tf_op | source)
XLA Modules:
  0.0 58.5 jit_solution(10594980884902161822)
XLA Ops:
  0.6 0.7 %copy.14.lengths_ref = s32[4,1]{1,0:T(4,128)S(1)} copy(s32[4,1]{0,1:T(1,128)} %param.11) | data formatting | bytes 32 | tf_op args[2]
  1.4 0.7 %copy.15.labels_ref = s32[4,1]{1,0:T(4,128)S(1)} copy(s32[4,1]{0,1:T(1,128)} %param.12) | data formatting | bytes 32 | tf_op args[3]
  2.1 0.7 %reduce = f32[1536]{0:T(1024)S(1)} reduce(f32[1,1536]{1,0:T(1,128)} %gain_ref.1, f32[]{:T(128)} %constant.7), dimensions={0}, to_apply=%param.13.reduce_sub_computation | reduce | bytes 12292 | tf_op args[4]
  2.8 0.1 reshape.21.gain_cut_ref
  2.9 1.0 %copy.16.cs_ref = bf16[768,29]{1,0:T(8,128)(2,1)S(1)} copy(bf16[768,29]{0,1:T(8,128)(2,1)} %param.17) | data formatting | bytes 89088 | tf_op args[8]
  3.9 0.0 copy-start
  3.9 0.7 %copy-done = f32[1,1536]{1,0:T(1,128)S(1)} copy-done((f32[1,1536]{1,0:T(1,128)S(1)}, f32[1,1536]{1,0:T(1,128)}, u32[]{:S(2)}) %copy-start) | copy-done | bytes 6168
  4.6 0.0 copy-start.1
  4.6 1.1 %copy-done.1 = bf16[1,1536,256]{2,1,0:T(8,128)(2,1)S(1)} copy-done((bf16[1,1536,256]{2,1,0:T(8,128)(2,1)S(1)}, bf16[1,1536,256]{2,1,0:T(8,128)(2,1)}, u32[]{:S(2)}) %copy-start.1) | copy-done | bytes 786456
  5.7 49.5 %shard_map.128 = (f32[96,256]{1,0:T(8,128)S(1)}, f32[96,256]{1,0:T(8,128)S(1)}, f32[1,96]{1,0:T(1,128)S(1)}, f32[768,48]{1,0:T(8,128)S(1)}, f32[48,29]{1,0:T(8,128)S(1)}) custom-call(s32[4,1]{1,0:T(4,128)S(1)} %copy.14.lengths_ref, s32[4,1]{1,0:T(4,128)S(1)} %copy.15.labels_ref, bf16[512,1536]{1,0:T(8,128)(2,1)} %bitcast.11, bf16[512,1536]{1,0:T(8,128)(2,1)} %bitcast.12, ...), custom_call_target="tpu_custom_call" | custom-call | flops 2415919104 | bytes 8388608 | tf_op jit(solution)/shard_map/pallas_call | solution.py:416
  55.2 0.7 %copy.18 = f32[48,29]{0,1:T(8,128)} copy(f32[48,29]{1,0:T(8,128)S(1)} %get-tuple-element.19) | data formatting | bytes 11136
  55.9 0.8 %copy.17 = f32[768,48]{0,1:T(8,128)} copy(f32[768,48]{1,0:T(8,128)S(1)} %get-tuple-element.18) | data formatting | bytes 294912
  56.7 0.6 %copy.22 = f32[1,96,256]{2,1,0:T(8,128)} copy(f32[1,96,256]{2,1,0:T(8,128)S(1)} %bitcast.9) | data formatting | bytes 196608
  57.3 0.6 %copy.23 = f32[1,256,96]{1,2,0:T(8,128)} copy(f32[1,256,96]{1,2,0:T(8,128)S(1)} %bitcast.8) | data formatting | bytes 196608
  57.9 0.5 copy.24
Async XLA Ops:
  3.9 0.7 %copy-start = (f32[1,1536]{1,0:T(1,128)S(1)}, f32[1,1536]{1,0:T(1,128)}, u32[]{:S(2)}) copy-start(f32[1,1536]{1,0:T(1,128)} %gain_ref.1) | copy-start | bytes 18436
  4.6 1.1 %copy-start.1 = (bf16[1,1536,256]{2,1,0:T(8,128)(2,1)S(1)}, bf16[1,1536,256]{2,1,0:T(8,128)(2,1)}, u32[]{:S(2)}) copy-start(bf16[1,1536,256]{2,1,0:T(8,128)(2,1)} %param.14) | copy-start | bytes 2359300

commit v2 on v1

--- a/solution.py
+++ b/solution.py
@@ -24,20 +24,19 @@
 
 def bit_orders(bits):
     near = list(range(bits))
-    return near, ([0] + near[2:] + [1] if bits > 1 else near)
+    return near, [0] + near[2:] + [1]
 
 
 def relay_kernel(
     sizes,
     lengths_ref,
     labels_ref,
-    x_ref,
-    g_ref,
-    gain_ref,
-    gain_cut_ref,
-    wd_ref,
-    wu_ref,
-    cf_ref,
+    x_hbm,
+    g_hbm,
+    gain_hbm,
+    wd_hbm,
+    wu_hbm,
+    cf_hbm,
     cs_ref,
     gwd_ref,
     gwu_ref,
@@ -48,6 +47,13 @@
 ):
     micro, length, bits, chunk = sizes
     (
+        x_ref,
+        g_ref,
+        gain_ref,
+        wd_ref,
+        wu_ref,
+        cf_ref,
+        gain_cut_ref,
         xn_ref,
         g0_ref,
         h_ref,
@@ -68,7 +74,9 @@
         last_ref,
         last_in_ref,
         *job_refs,
+        load_sems,
         x_sems,
+        p_sems,
         ag_sems,
         rs_sems,
     ) = scratch
@@ -76,7 +84,7 @@
     tokens, features = x_ref.shape
     rank = wd_ref.shape[1]
     band, hidden_width = cf_ref.shape
-    languages = cs_ref.shape[1]
+    languages = cs_ref.shape[0]
     cut = features // dp
     section = lax.axis_index("section")
     replica = lax.axis_index("dp")
@@ -86,10 +94,29 @@
         mine = lax.rem(replica // (1 << bit), 2)
         return mine, (section, replica + (1 - 2 * mine) * (1 << bit))
 
-    orders = bit_orders(bits)
-    job_order = (orders[0], orders[1], orders[0])
-    cuts = [job_refs[job * 2 * bits : job * 2 * bits + bits] for job in range(3)]
-    lands = [job_refs[job * 2 * bits + bits : (job + 1) * 2 * bits] for job in range(3)]
+    job_order = bit_orders(bits) * 3
+    cuts = [job_refs[job * 2 * bits : job * 2 * bits + bits] for job in range(6)]
+    lands = [job_refs[job * 2 * bits + bits : (job + 1) * 2 * bits] for job in range(6)]
+    loads = [
+        pltpu.make_async_copy(src, dst, load_sems.at[slot])
+        for slot, (src, dst) in enumerate(
+            (
+                (x_hbm, x_ref),
+                (wd_hbm, wd_ref),
+                (gain_hbm, gain_ref),
+                (cf_hbm, cf_ref),
+                (g_hbm, g_ref),
+                (wu_hbm, wu_ref),
+            )
+        )
+    ]
+    for load in loads[:4]:
+        load.start()
+
+    @pl.when(section == 1)
+    def _():
+        loads[4].start()
+        loads[5].start()
 
     def x_copy(slot, src, dst, device):
         return pltpu.make_async_remote_copy(
@@ -103,7 +130,7 @@
 
     core, beside = peer(0)
     half_rank = rank // 2
-    my_half = wu_ref.at[pl.ds(pl.multiple_of(core * half_rank, half_rank), half_rank)]
+    my_half = wu_hbm.at[pl.ds(pl.multiple_of(core * half_rank, half_rank), half_rank)]
     my_half_in = wu_in_ref.at[pl.ds(pl.multiple_of(core * half_rank, half_rank), half_rank)]
     up_across = x_copy(0, my_half, my_half_in, across)
     up_beside = x_copy(1, my_half_in, my_half_in, beside)
@@ -111,8 +138,20 @@
     pre_across = x_copy(3, pre_ref, pre_in_ref, across)
     gn_across = x_copy(4, gn_ref, gn_in_ref, across)
     h_across = x_copy(5, h_ref, h0_ref, across)
-    p_across = x_copy(6, p_ref, p_in_ref, across)
-    last_across = x_copy(7, last_ref, last_in_ref, across)
+    last_across = [
+        x_copy(6 + side, last_ref.at[side], last_in_ref.at[side], across) for side in range(2)
+    ]
+
+    def p_copy(m):
+        rows = pl.ds(m * length, length)
+        return pltpu.make_async_remote_copy(
+            src_ref=p_ref.at[rows],
+            dst_ref=p_in_ref.at[rows],
+            send_sem=p_sems.at[2 * m],
+            recv_sem=p_sems.at[2 * m + 1],
+            device_id=across,
+            device_id_type=MESH,
+        )
 
     def ag_copy(step):
         count = 1 << step
@@ -148,7 +187,7 @@
         cuts[job][step + 1][...] = rs_take(job, step).astype(BF16)
         rs_copy(job, step + 1).start()
 
-    def fill(job, left_ref, right_ref, extra=None):
+    def fill(matrix, left_ref, right_ref, extra=None):
         group = 4 * cut
         for part in range(features // group):
             columns = pl.ds(part * group, group)
@@ -160,16 +199,33 @@
             product = product.astype(BF16)
             for inner in range(4):
                 target = part * 4 + inner
-                place = 0
-                for step, bit in enumerate(job_order[job]):
-                    place += ((target >> bit) & 1) << (bits - 1 - step)
-                cuts[job][0][place] = product[inner * cut : (inner + 1) * cut]
+                for side in range(2):
+                    job = 2 * matrix + side
+                    place = 0
+                    for step, bit in enumerate(job_order[job]):
+                        place += ((target >> bit) & 1) << (bits - 1 - step)
+                    cuts[job][0][place] = product[
+                        inner * cut : (inner + 1) * cut,
+                        side * half_rank : (side + 1) * half_rank,
+                    ]
+        for side in range(2):
+            rs_copy(2 * matrix + side, 0).start()
+
+    def advance(matrix, step):
+        rs_step(2 * matrix, step)
+        rs_step(2 * matrix + 1, step)
 
     barrier = pltpu.get_barrier_semaphore()
     pl.semaphore_signal(barrier, inc=1, device_id=across, device_id_type=MESH)
     for bit in range(bits):
         pl.semaphore_signal(barrier, inc=1, device_id=peer(bit)[1], device_id_type=MESH)
     pl.semaphore_wait(barrier, bits + 1)
+
+    @pl.when(section == 0)
+    def _():
+        up_across.start()
+
+    loads[0].wait()
 
     row_of = lax.broadcasted_iota(jnp.int32, (PAD, tokens), 0)
     token_of = lax.broadcasted_iota(jnp.int32, (PAD, tokens), 1)
@@ -178,11 +234,11 @@
     lengths = jnp.ones((PAD, 1), F32)
     labels = jnp.full((PAD, 1), -1, jnp.int32)
     for m in range(micro):
-        seq = lengths_ref[m, 0]
+        seq = lengths_ref[0, m]
         inside = (row_of == m) & (token_of >= m * length) & (token_of < m * length + seq)
         valid = jnp.where(inside, 1.0, valid)
         lengths = jnp.where(pad_rows == m, seq.astype(F32), lengths)
-        labels = jnp.where(pad_rows == m, labels_ref[m, 0], labels)
+        labels = jnp.where(pad_rows == m, labels_ref[0, m], labels)
     valid = valid.astype(BF16)
 
     def normalised(rows):
@@ -198,14 +254,14 @@
 
     @pl.when(section == 0)
     def _():
-        up_across.start()
+        loads[1].wait()
+        loads[2].wait()
 
         @pl.loop(0, tokens // chunk)
         def _(index):
             rows = pl.ds(pl.multiple_of(index * chunk, chunk), chunk)
             slope_ref[rows, :] = normalised(rows)[2]
 
-        h_across.start()
         pool_across.wait_recv()
 
     @pl.when(section == 1)
@@ -218,13 +274,17 @@
     pooled_inv = lax.rsqrt(jnp.mean(pooled * pooled, axis=-1, keepdims=True) + EPSILON)
     pooled_unit = pooled * pooled_inv
     pooled_normed = jnp.where(section == 0, pooled_unit[:, :band], pooled_unit[:, band:])
+    loads[3].wait()
     pre_ref[...] = contract(pooled_normed.astype(BF16), cf_ref[...], 1, 0)
     pre_across.start()
     cs_pad_ref[...] = jnp.zeros(cs_pad_ref.shape, BF16)
-    cs_pad_ref[:, :languages] = cs_ref[...]
+    cs_pad_ref[:languages, :] = cs_ref[...]
 
     @pl.when(section == 1)
     def _():
+        for slot in (1, 2, 4, 5):
+            loads[slot].wait()
+
         @pl.loop(0, tokens // chunk)
         def _(index):
             rows = pl.ds(pl.multiple_of(index * chunk, chunk), chunk)
@@ -240,9 +300,7 @@
             ).astype(BF16)
 
         fill(0, xn_ref, da_ref)
-        rs_copy(0, 0).start()
         fill(1, g_ref, h_ref)
-        rs_copy(1, 0).start()
         up_across.wait_recv()
         up_beside.start()
 
@@ -250,19 +308,23 @@
     pre = pre_ref[...] + pre_in_ref[...]
     sigma = jax.nn.sigmoid(pre)
     hidden = (pre * sigma).astype(BF16)
-    logits = contract(hidden, cs_pad_ref[...], 1, 0)
+    logits = contract(hidden, cs_pad_ref[...], 1, 1)
     language = lax.broadcasted_iota(jnp.int32, (PAD, LANES), 1)
     exponent = jnp.where(language < languages, jnp.exp(logits), 0.0)
     probabilities = exponent / jnp.sum(exponent, axis=-1, keepdims=True)
     onehot = jnp.where(language == labels, 1.0, 0.0)
     grad_logits = (probabilities - onehot).astype(BF16)
-    grad_hidden = contract(grad_logits, cs_pad_ref[...], 1, 1)
+    grad_hidden = contract(grad_logits, cs_pad_ref[...], 1, 0)
     grad_pre = (grad_hidden * (sigma * (1.0 + pre * (1.0 - sigma)))).astype(BF16)
     gn_ref[...] = contract(grad_pre, cf_ref[...], 1, 1)
 
     @pl.when(section == 0)
     def _():
         gn_across.start()
+        up_across.wait_send()
+        h_across.start()
+        for target in range(dp):
+            gain_cut_ref[target : target + 1, :] = gain_ref[:, target * cut : (target + 1) * cut]
 
     pack32_ref[...] = jnp.zeros(pack32_ref.shape, F32)
     pack32_ref[0:micro, :band] = pooled_normed[:micro]
@@ -274,6 +336,8 @@
 
     @pl.when(section == 1)
     def _():
+        for target in range(dp):
+            gain_cut_ref[target : target + 1, :] = gain_ref[:, target * cut : (target + 1) * cut]
         gn_across.wait_recv()
         grad_normed = jnp.concatenate([gn_in_ref[...], gn_ref[...]], axis=1)
         tilt = jnp.mean(grad_normed * pooled_unit, axis=-1, keepdims=True)
@@ -284,16 +348,15 @@
         up_reversal = contract(reversal, wu_in_ref[...], 1, 1)
         for m in range(micro):
             rows = pl.ds(m * length, length)
-            inside = lax.broadcasted_iota(jnp.int32, (length, 1), 0) < lengths_ref[m, 0]
+            inside = lax.broadcasted_iota(jnp.int32, (length, 1), 0) < lengths_ref[0, m]
             extra = jnp.where(inside, up_reversal[m : m + 1], 0.0)
             p_ref[rows, :] = (contract(g0_ref[rows, :], wu_in_ref[...], 1, 1) + extra).astype(BF16)
-        p_across.start()
-        rs_step(0, 0)
-        rs_step(1, 0)
+            p_copy(m).start()
+        advance(0, 0)
+        advance(1, 0)
         h_across.wait_recv()
         masked_h = contract(valid, h0_ref[...], 1, 0).astype(BF16)
         fill(2, g0_ref, h0_ref, (reversal, masked_h))
-        rs_copy(2, 0).start()
 
     def ag_step(step):
         ag_copy(step).wait_recv()
@@ -317,11 +380,13 @@
         moved_pre = jnp.where(place < micro, moved_pre, 0.0).astype(BF16)
         moved_logits = contract(shift, blocks[:, :LANES], 1, 0).astype(BF16)
         hidden_own = jnp.where((place >= micro) & (place < 2 * micro), picked, 0.0).astype(BF16)
-        first_ref[...] = contract(blocks[:, :band], moved_pre, 0, 0)[:, :own]
-        second_ref[...] = contract(hidden_own, moved_logits, 0, 0)[:own, :languages]
+        first_ref[...] = contract(moved_pre, blocks[:, :band], 0, 0)[:own]
+        second_ref[...] = contract(moved_logits, hidden_own, 0, 0)[:languages, :own]
 
     def finish_down():
-        reduced = rs_take(0, bits - 1)[0]
+        reduced = jnp.concatenate(
+            [rs_take(0, bits - 1)[0], rs_take(1, bits - 1)[0]], axis=1
+        )
         gwd_ref[...] = reduced
         start = pl.multiple_of(replica * cut, cut)
         weighted = reduced * wd_ref[pl.ds(start, cut), :].astype(F32)
@@ -336,42 +401,49 @@
 
     @pl.when(section == 1)
     def _():
-        for step in range(bits):
+        ag_step(0)
+        for step in range(1, bits):
+            if step + 1 < bits:
+                advance(0, step)
+                advance(1, step)
             ag_step(step)
-            if step + 1 < bits:
-                rs_step(2, step)
-            if step + 2 < bits:
-                rs_step(0, step + 1)
-                rs_step(1, step + 1)
-        last_ref[...] = rs_take(2, bits - 1)[0]
-        last_across.start()
+            if step == 1:
+                advance(2, 0)
+        for step in range(1, bits - 1):
+            advance(2, step)
+        critic_outputs()
+        for side in range(2):
+            last_ref[side] = rs_take(4 + side, bits - 1)[0]
+            last_across[side].start()
         finish_down()
-        gwu_ref[...] = rs_take(1, bits - 1)[0]
-        critic_outputs()
+        for side in range(2):
+            gwu_ref[:, side * half_rank : (side + 1) * half_rank] = rs_take(2 + side, bits - 1)[0]
 
     @pl.when(section == 0)
     def _():
         for step in range(bits):
             ag_step(step)
         critic_outputs()
-        p_across.wait_recv()
-        da_ref[...] = (p_in_ref[...].astype(F32) * slope_ref[...]).astype(BF16)
+        for m in range(micro):
+            p_copy(m).wait_recv()
+            rows = pl.ds(m * length, length)
+            da_ref[rows, :] = (p_in_ref[rows, :].astype(F32) * slope_ref[rows, :]).astype(BF16)
         fill(0, xn_ref, da_ref)
-        rs_copy(0, 0).start()
         for step in range(bits - 1):
-            rs_step(0, step)
+            advance(0, step)
         finish_down()
-        last_across.wait_recv()
-        gwu_ref[...] = last_in_ref[...]
+        for side in range(2):
+            last_across[side].wait_recv()
+            gwu_ref[:, side * half_rank : (side + 1) * half_rank] = last_in_ref[side]
 
     pre_across.wait_send()
     for step in range(bits):
         ag_copy(step).wait_send()
         rs_copy(0, step).wait_send()
+        rs_copy(1, step).wait_send()
 
     @pl.when(section == 0)
     def _():
-        up_across.wait_send()
         h_across.wait_send()
         gn_across.wait_send()
 
@@ -379,11 +451,26 @@
     def _():
         up_beside.wait_send()
         pool_across.wait_send()
-        p_across.wait_send()
-        last_across.wait_send()
+        for m in range(micro):
+            p_copy(m).wait_send()
+        for side in range(2):
+            last_across[side].wait_send()
         for step in range(bits):
-            rs_copy(1, step).wait_send()
-            rs_copy(2, step).wait_send()
+            for job in range(2, 6):
+                rs_copy(job, step).wait_send()
+
+
+def hand_over(*refs):
+    sems = refs[-1]
+    count = (len(refs) - 1) // 2
+    copies = [
+        pltpu.make_async_copy(refs[slot], refs[count + slot], sems.at[slot])
+        for slot in range(count)
+    ]
+    for copy in copies:
+        copy.start()
+    for copy in copies:
+        copy.wait()
 
 
 def fused_body(
@@ -408,23 +495,32 @@
     width = max(band, hidden_width)
     chunk = min(2 * length, tokens)
     jobs = []
-    for _ in range(3):
-        jobs += [pltpu.VMEM((dp >> step, cut, rank), BF16) for step in range(bits)]
-        jobs += [pltpu.VMEM((dp >> (step + 1), cut, rank), BF16) for step in range(bits)]
+    for _ in range(6):
+        jobs += [pltpu.VMEM((dp >> step, cut, rank // 2), BF16) for step in range(bits)]
+        jobs += [pltpu.VMEM((dp >> (step + 1), cut, rank // 2), BF16) for step in range(bits)]
     vmem = pl.BlockSpec(memory_space=pltpu.VMEM)
     smem = pl.BlockSpec(memory_space=pltpu.SMEM)
-    gwd, gwu, gain, first, second = pl.pallas_call(
+    anywhere = pl.BlockSpec(memory_space=pl.ANY)
+    results = (
+        jax.ShapeDtypeStruct((cut, rank), F32),
+        jax.ShapeDtypeStruct((cut, rank), F32),
+        jax.ShapeDtypeStruct((1, cut), F32),
+        jax.ShapeDtypeStruct((hidden_width // dp, band), F32),
+        jax.ShapeDtypeStruct((languages, hidden_width // dp), F32),
+    )
+    held = pl.pallas_call(
         functools.partial(relay_kernel, (micro, length, bits, chunk)),
-        out_shape=(
-            jax.ShapeDtypeStruct((cut, rank), F32),
-            jax.ShapeDtypeStruct((cut, rank), F32),
-            jax.ShapeDtypeStruct((1, cut), F32),
-            jax.ShapeDtypeStruct((band, hidden_width // dp), F32),
-            jax.ShapeDtypeStruct((hidden_width // dp, languages), F32),
-        ),
-        in_specs=[smem, smem] + [vmem] * 8,
+        out_shape=results,
+        in_specs=[smem, smem] + [anywhere] * 6 + [vmem],
         out_specs=(vmem,) * 5,
         scratch_shapes=[
+            pltpu.VMEM((tokens, features), BF16),
+            pltpu.VMEM((tokens, features), BF16),
+            pltpu.VMEM((1, features), F32),
+            pltpu.VMEM((features, rank), BF16),
+            pltpu.VMEM((rank, features), BF16),
+            pltpu.VMEM((band, hidden_width), BF16),
+            pltpu.VMEM((dp, cut), F32),
             pltpu.VMEM((tokens, features), BF16),
             pltpu.VMEM((tokens, features), BF16),
             pltpu.VMEM((tokens, rank), BF16),
@@ -439,35 +535,43 @@
             pltpu.VMEM((PAD, hidden_width), F32),
             pltpu.VMEM((PAD, band), F32),
             pltpu.VMEM((PAD, band), F32),
-            pltpu.VMEM((hidden_width, LANES), BF16),
+            pltpu.VMEM((LANES, hidden_width), BF16),
             pltpu.VMEM((PAD, width), F32),
             pltpu.VMEM((dp, PAD, width), BF16),
-            pltpu.VMEM((cut, rank), F32),
-            pltpu.VMEM((cut, rank), F32),
+            pltpu.VMEM((2, cut, rank // 2), F32),
+            pltpu.VMEM((2, cut, rank // 2), F32),
             *jobs,
+            pltpu.SemaphoreType.DMA((6,)),
             pltpu.SemaphoreType.DMA((16,)),
+            pltpu.SemaphoreType.DMA((2 * micro,)),
             pltpu.SemaphoreType.DMA((2 * bits,)),
-            pltpu.SemaphoreType.DMA((6 * bits,)),
+            pltpu.SemaphoreType.DMA((12 * bits,)),
         ],
         compiler_params=pltpu.CompilerParams(
-            collective_id=0, has_side_effects=True, vmem_limit_bytes=52 * 2**20
+            collective_id=0, has_side_effects=True, vmem_limit_bytes=58 * 2**20
         ),
         cost_estimate=pl.CostEstimate(
             flops=12 * tokens * features * rank, bytes_accessed=8 * 2**20, transcendentals=0
         ),
     )(
-        seq_lengths,
-        lang_labels,
+        seq_lengths.T,
+        lang_labels.T,
         section_in.reshape(tokens, features),
         top_grad.reshape(tokens, features),
         norm_gain,
-        norm_gain.reshape(dp, cut),
         w_down[0],
         w_up[0],
         critic_first,
-        critic_second,
-    )
-    return (gwd[None], gwu.T[None], gain, first, second)
+        critic_second.T,
+    )
+    gwd, gwu, gain, first, second = pl.pallas_call(
+        hand_over,
+        out_shape=results,
+        in_specs=[anywhere] * 5,
+        out_specs=(anywhere,) * 5,
+        scratch_shapes=[pltpu.SemaphoreType.DMA((5,))],
+    )(*held)
+    return (gwd[None], gwu.T[None], gain, first.T, second.T)
 
 
 def from_root(array, axis, root):
@@ -645,7 +749,8 @@
             and replicas >= 4
             and replicas & (replicas - 1) == 0
             and micro * 4 == PAD
-            and args[4].shape[1] % (replicas * PAD) == 0
+            and args[4].shape[1] % (replicas * 2 * PAD) == 0
+            and args[5].shape[2] % (2 * LANES) == 0
         )
         return placed(mesh, fused_body if fits else body)(*args)
 

time: 58.8 us -> 60.6 us (1.031)
  Pallas kernels: 49.5 us -> 59.8 us
  local copies, waits for them, and re-layouts: 7.63 us -> 0 us
  other arithmetic: 0.71 us -> 0 us
    pallas_call x0 -> x1, Pallas kernels: none -> 12 us  [fused_body(): pl.pallas_call(hand_over, out_shape=results, in_specs=[anywhere] * 5, out...]
    unnamed x12 -> x0, local copies, waits for them, and re-layouts: 7.56 us -> none
    pallas_call x1, Pallas kernels: 49.5 us -> 47.7 us  [fused_body(): pl.pallas_call(functools.partial(relay_kernel, (micro, length, bits, chun...]
    unnamed x1 -> x0, other arithmetic: 0.71 us -> none
where the time goes in v2:
time: 60.6 us; the launch traced here: 60.4 us
  Pallas kernels  59.8 us (99%)
  between operations  0.64 us (1%)
    pallas_call x1, Pallas kernels, fused_body(): pl.pallas_call(functools.partial(relay_kernel, (micro, length, bits, chun...  47.7 us
    pallas_call x1, Pallas kernels, fused_body(): pl.pallas_call(hand_over, out_shape=results, in_specs=[anywhere] * 5, out...  12 us

profile of v2, /device:TPU:0, one launch (start us, length us, event | category | flops | bytes accessed | tf_op | source)
XLA Modules:
  0.0 60.4 jit_solution(997111413602612175)
XLA Ops:
  0.6 47.7 %shard_map.128 = (f32[96,256]{1,0:T(8,128)}, f32[96,256]{1,0:T(8,128)}, f32[1,96]{1,0:T(1,128)}, f32[48,768]{1,0:T(8,128)}, f32[29,48]{1,0:T(8,128)}) custom-call(s32[1,4]{1,0:T(1,128)} %bitcast.22, s32[1,4]{1,0:T(1,128)} %bitcast.23, bf16[512,1536]{1,0:T(8,128)(2,1)} %bitcast.13, bf16[512,1536]{1,0:T(8,128)(2,1)} %bitcast.14, f32[1,1536]{1,0:T(1,128)} %gain_hbm.1, ...), custom_call_target="tpu_custom_call" | custom-call | flops 2415919104 | bytes 8388608 | tf_op jit(solution)/shard_map/pallas_call | solution.py:511
  48.4 12.0 %shard_map.129 = (f32[96,256]{1,0:T(8,128)}, f32[96,256]{1,0:T(8,128)}, f32[1,96]{1,0:T(1,128)}, f32[48,768]{1,0:T(8,128)}, f32[29,48]{1,0:T(8,128)}) custom-call(f32[96,256]{1,0:T(8,128)} %get-tuple-element.15.refs_0_, f32[96,256]{1,0:T(8,128)} %get-tuple-element.16.refs_1_, f32[1,96]{1,0:T(1,128)} %get-tuple-element.17.refs_2_, ...), custom_call_target="tpu_custom_call" | custom-call | tf_op jit(solution)/shard_map/pallas_call | solution.py:567
